TPU v7x, 32 devices: a whole 2x2x4 slice. The times are simulated.
32 devices in a mesh: gx: 4 (over y, x), gy: 8 (over z, core).
Axes of the slice: x: 2, y: 2, z: 4, core: 2. Of those that a mesh axis runs over, the one named last changes fastest.
Arguments:
- volume: bfloat16 [32, 8, 256, 256], P(None, 'gx', 'gy'), may hold values from -6 to 6
- conv1_weight: bfloat16 [3, 3, 3, 32, 64], replicated, may hold values from -0.21875 to 0.21875
- conv1_bias: float32 [64], replicated, may hold values from -3 to 3
- conv2_weight: bfloat16 [3, 3, 3, 64, 128], replicated, may hold values from -0.15625 to 0.15625
- conv2_bias: float32 [128], replicated, may hold values from -3 to 3
Outputs:
- activation: bfloat16 [4, 128, 128, 128], P('gx', 'gy')
All inputs are finite; a program needn't handle non-finite values.
Results may differ from a plain program's by a relative error of at most 0.0045.
Values may be sent and summed in bfloat16 or wider, within the bound.
A program may use at most 256 MiB of HBM per device.

v0:
```python
import jax
import jax.numpy as jnp
from jax import lax
from jax.sharding import PartitionSpec as P

leak_slope = 0.3


def shifted(value, axis, steps):
    count = lax.axis_size(axis)
    initial, last = (max(0, -steps), min(count, count - steps))
    return lax.ppermute(value, axis, [(source, source + steps) for source in range(initial, last)])


def leaky(values):
    return jnp.where(values > 0, values, leak_slope * values)


def on_device(volume, conv1_weight, conv1_bias, conv2_weight, conv2_bias):
    x_edge = shifted(volume[:, -1:, :, :], "gx", 1)
    grown_x = jnp.concatenate([x_edge, volume], axis=1)
    y_edge = shifted(grown_x[:, :, -1:, :], "gy", 1)
    grown = jnp.concatenate([y_edge, grown_x], axis=2)
    first = lax.conv_general_dilated(
        grown[None],
        conv1_weight,
        (2, 2, 2),
        ((0, 0), (0, 0), (1, 0)),
        dimension_numbers=("NCDHW", "DHWIO", "NCDHW"),
        preferred_element_type=jnp.float32,
    )[0]
    feature = leaky(first + conv1_bias[:, None, None, None]).astype(jnp.bfloat16)
    planes = feature.shape[1]
    groups = lax.axis_size("gx")
    filter_groups = lax.axis_size("gy")
    group_width = conv2_weight.shape[3] // groups
    filters_all = conv2_weight.shape[4]
    filter_width = filters_all // filter_groups
    moved = lax.all_to_all(feature, "gx", split_axis=0, concat_axis=1, tiled=True)
    gathered = lax.all_gather(moved, "gy", axis=2, tiled=True)
    padded = jnp.pad(gathered, ((0, 0), (1, 1), (0, 0), (0, 0)))
    group_index = lax.axis_index("gx")
    filter_index = lax.axis_index("gy")
    zero = jnp.zeros((), jnp.int32)
    kernel = lax.dynamic_slice(
        conv2_weight,
        (zero, zero, zero, group_index * group_width, filter_index * filter_width),
        (3, 3, 3, group_width, filter_width),
    )
    slab = lax.slice_in_dim(padded, 0, lax.axis_size("gx") * planes + 2, axis=1)
    term = lax.conv_general_dilated(
        slab[None],
        kernel,
        (1, 1, 1),
        ((0, 0), (1, 1), (1, 1)),
        dimension_numbers=("NCDHW", "DHWIO", "DNCHW"),
        preferred_element_type=jnp.float32,
    )
    summed = lax.psum_scatter(term[:, 0], "gx", scatter_dimension=0, tiled=True)
    bias_part = lax.dynamic_slice_in_dim(conv2_bias, filter_index * filter_width, filter_width)
    return leaky(summed + bias_part[None, :, None, None]).astype(jnp.bfloat16)


def solution(mesh):
    return jax.shard_map(
        on_device,
        mesh=mesh,
        in_specs=(P(None, "gx", "gy", None), P(), P(), P(), P()),
        out_specs=P("gx", "gy", None, None),
        check_vma=False,
    )
```

profile of v0, /device:TPU:5, one launch (start us, length us, event | category | flops | bytes accessed | tf_op | source)
XLA Modules:
  0.0 276.6 jit_solution(18355096036190895998)
XLA Ops:
  6.5 0.0 copy-start
  6.5 0.0 all-gather.3.cloned.1.call-start
  6.5 1.1 slice.6
  7.7 3.1 %collective-permute-start = (bf16[32,1,32,256]{3,2,1,0:T(8,128)(2,1)S(1)}, bf16[32,1,32,256]{3,2,1,0:T(8,128)(2,1)S(1)}, u32[]{:S(2)}, u32[]{:S(2)}) collective-permute-start(bf16[32,1,32,256]{3,2,1,0:T(8,128)(2,1)S(1)} %slice.6), channel_id=1, source_target_pairs={{0,8},{8,16},{16,24},{1,9},{9,17},{17,25},{2,10},{10,18},{18,26},{... | collective-permute-start | bytes 1572872 | tf_op jit(solution)/shard_map/ppermute | solution.py:12
  10.8 12.5 %collective-permute-done = bf16[32,1,32,256]{3,2,1,0:T(8,128)(2,1)S(1)} collective-permute-done((bf16[32,1,32,256]{3,2,1,0:T(8,128)(2,1)S(1)}, bf16[32,1,32,256]{3,2,1,0:T(8,128)(2,1)S(1)}, u32[]{:S(2)}, u32[]{:S(2)}) %collective-permute-start) | collective-permute-done | bytes 524320 | tf_op jit(solution)/shard_map/ppermute | solution.py:12
  23.3 1.3 constant_dynamic-update-slice_fusion
  24.6 0.1 slice.12
  24.7 4.6 %collective-permute-start.1 = (bf16[32,3,1,256]{3,2,1,0:T(2,128)(2,1)S(1)}, bf16[32,3,1,256]{3,2,1,0:T(2,128)(2,1)S(1)}, u32[]{:S(2)}, u32[]{:S(2)}) collective-permute-start(bf16[32,3,1,256]{3,2,1,0:T(2,128)(2,1)S(1)} %slice.12), channel_id=1, source_target_pairs={{0,1},{1,2},{2,3},{3,4},{4,5},{5,6},{6,7},{8,9},{9,10},{10,11},{11... | collective-permute-start | bytes 147464 | tf_op jit(solution)/shard_map/ppermute | solution.py:12
  29.4 1.6 collective-permute-done.1
  31.0 1.2 maximum_bitcast_fusion
  32.1 1.4 pad.5
  33.5 7.3 %reshape.60 = bf16[32,3,33,1,8,34]{5,4,2,1,0,3:T(8,128)(2,1)} reshape(bf16[32,3,33,1,272]{4,2,1,0,3:T(8,128)(2,1)S(1)} %pad.5) | data formatting | bytes 3446784 | tf_op jit(solution)/shard_map/conv_general_dilated | solution.py:24
  40.8 0.0 copy-start.3
  40.8 0.0 copy-start.5
  40.8 11.5 %copy.39 = bf16[32,3,33,1,8,34]{0,4,5,2,1,3:T(8,128)(2,1)} copy(bf16[32,3,33,1,8,34]{5,4,2,1,0,3:T(8,128)(2,1)} %reshape.60) | data formatting | bytes 3446784 | tf_op jit(solution)/shard_map/conv_general_dilated | solution.py:24
  52.3 1.1 slice.13
  53.4 0.0 copy-done.3
  53.4 0.0 copy-done.5
  53.4 0.0 copy-start.2
  53.5 6.0 %fusion.17 = f32[1,16,8,17,64]{4,2,3,1,0:T(8,128)S(1)} fusion(bf16[3,3,3,32,64]{4,3,2,1,0:T(8,128)(2,1)S(1)} %copy-done.3, bf16[32,3,33,1,7,2]{0,4,5,2,1,3:T(8,128)(2,1)S(1)} %slice.13, bf16[32,3,33,1,8,34]{0,4,5,2,1,3:T(8,128)(2,1)} %copy.39, pred[8,17]{0,1:T(8,128)(4,1)S(1)} %copy-done.5), kind=kOutput, calls=%fused_computation.21 | convolution fusion | flops 246261760 | bytes 2479880 | tf_op jit(solution)/shard_map/conv_general_dilated | solution.py:24
  59.4 0.2 copy.40
  59.6 0.1 slice.14
  59.7 0.6 copy.49
  60.3 0.0 copy-done.2
  60.3 0.2 fusion.21
  60.5 6.4 %all_to_all.18 = bf16[64,1,16,128]{3,2,1,0:T(8,128)(2,1)} all-to-all(bf16[64,1,16,128]{3,2,1,0:T(8,128)(2,1)S(1)} %fusion.21), channel_id=1, replica_groups=mesh['gx'=4,'gy'=8] {'gx'}, dimensions={0} | all-to-all | bytes 524288 | tf_op jit(solution)/shard_map/all_to_all | solution.py:39
  66.9 0.0 all-gather.3.cloned.1.call-update
  66.9 0.0 reduce-scatter.4.cloned.1.call-start
  67.0 33.3 %all-gather.3.cloned.1.call-done = bf16[16,4,1,128,128]{4,3,0,1,2:T(8,128)(2,1)} async-done(((bf16[16,4,1,16,128]{4,3,0,1,2:T(8,128)(2,1)}), bf16[16,4,1,128,128]{4,3,0,1,2:T(8,128)(2,1)}) %all-gather.3.cloned.1.call-update) | async-done | bytes 2097168 | tf_op jit(solution)/shard_map/all_gather | solution.py:40
  100.3 3.8 %pad_bitcast_fusion = bf16[16,6,128,1,128]{4,2,0,1,3:T(8,128)(2,1)} fusion(bf16[16,4,128,128]{3,2,0,1:T(8,128)(2,1)} %bitcast.38), kind=kLoop, calls=%fused_computation.17 | loop fusion | bytes 5242880 | tf_op jit(solution)/shard_map/broadcast_in_dim | solution.py:52
  104.1 5.0 %copy.50 = bf16[16,6,128,1,128]{2,0,4,1,3:T(8,128)(2,1)} copy(bf16[16,6,128,1,128]{4,2,0,1,3:T(8,128)(2,1)} %pad_bitcast_fusion) | data formatting | bytes 6291456
  109.1 4.1 %pad.7.clone = bf16[16,6,128,1,136]{2,0,4,1,3:T(8,128)(2,1)} pad(bf16[16,6,128,1,128]{2,0,4,1,3:T(8,128)(2,1)} %copy.50, bf16[]{:T(256)} %constant.4.clone.1), padding=0_0x0_0x0_0x0_0x1_7 | pad | bytes 6488066 | tf_op jit(solution)/shard_map/broadcast_in_dim | solution.py:52
  113.2 22.5 %copy.44 = bf16[16,6,128,1,8,17]{0,4,5,2,1,3:T(8,128)(2,1)} copy(bf16[16,6,128,1,8,17]{2,0,5,4,1,3:T(8,128)(2,1)} %bitcast.36) | data formatting | bytes 6684672 | tf_op jit(solution)/shard_map/conv_general_dilated | solution.py:51
  135.7 2.8 %slice.15 = bf16[16,6,128,1,7,2]{0,4,5,2,1,3:T(8,128)(2,1)S(1)} slice(bf16[16,6,128,1,8,17]{0,4,5,2,1,3:T(8,128)(2,1)} %copy.44), slice={[0:16], [0:6], [0:128], [0:1], [1:8], [0:2]} | slice | bytes 688128 | tf_op jit(solution)/shard_map/conv_general_dilated | solution.py:51
  138.5 0.0 copy-done
  138.5 49.9 %broadcast_select_fusion = f32[4,128,8,17,16]{4,2,3,1,0:T(8,128)} fusion(pred[8,17]{0,1:T(8,128)(4,1)S(1)} %copy-done.5, bf16[16,6,128,1,7,2]{0,4,5,2,1,3:T(8,128)(2,1)S(1)} %slice.15, bf16[16,6,128,1,8,17]{0,4,5,2,1,3:T(8,128)(2,1)} %copy.44, bf16[3,3,3,64,128]{4,3,2,1,0:T(8,128)(2,1)S(1)} %copy-done, s32[]{:T(128)S(6)} %select_n.24, s32[]{:T(128)S(6)} %select_n.25), kind=kOutput, calls=%fused_computation.8 | convolution fusion | flops 969900032 | bytes 11058184 | tf_op jit(solution)/shard_map/conv_general_dilated | solution.py:51
  188.4 22.4 %copy.45 = f32[4,128,8,17,16]{1,4,3,2,0:T(8,128)} copy(f32[4,128,8,17,16]{4,2,3,1,0:T(8,128)} %broadcast_select_fusion) | data formatting | bytes 8912896 | tf_op jit(solution)/shard_map/conv_general_dilated | solution.py:51
  210.8 0.0 copy-start.4
  210.8 0.0 copy-start.1
  210.8 4.6 %slice_bitcast_fusion = f32[4,16,128,128]{2,1,3,0:T(8,128)} fusion(f32[4,128,1,136,16]{1,4,3,2,0:T(8,128)} %bitcast.35), kind=kLoop, calls=%fused_computation.15 | loop fusion | bytes 8388608 | tf_op jit(solution)/shard_map/squeeze | solution.py:59
  215.4 0.0 reduce-scatter.4.cloned.1.call-update
  215.4 0.0 copy-done.4
  215.4 0.1 dynamic_slice.7
  215.5 51.6 %reduce-scatter.4.cloned.1.call-done = f32[1,16,128,128]{2,1,3,0:T(8,128)} async-done(((f32[4,16,128,128]{2,1,3,0:T(8,128)}), f32[1,16,128,128]{2,1,3,0:T(8,128)}) %reduce-scatter.4.cloned.1.call-update) | async-done | bytes 1048592
  267.1 1.5 fusion.20
  268.5 1.2 copy.46
  269.8 0.0 copy-done.1
  (1 shorter events, 0.0 us)
Async XLA Ops:
  6.5 132.0 %copy-start = (bf16[3,3,3,64,128]{4,3,2,1,0:T(8,128)(2,1)S(1)}, bf16[3,3,3,64,128]{4,3,2,1,0:T(8,128)(2,1)}, u32[]{:S(2)}) copy-start(bf16[3,3,3,64,128]{4,3,2,1,0:T(8,128)(2,1)} %param.8) | copy-start | bytes 1327108
  6.5 93.8 %all-gather.3.cloned.1.call-start = ((), (), s32[]{:S(2)}) async-start(), calls=%async_computation.2 | async-start | bytes 2359296 | tf_op jit(solution)/shard_map/all_gather | solution.py:40
  7.7 15.6 %collective-permute-start = (bf16[32,1,32,256]{3,2,1,0:T(8,128)(2,1)S(1)}, bf16[32,1,32,256]{3,2,1,0:T(8,128)(2,1)S(1)}, u32[]{:S(2)}, u32[]{:S(2)}) collective-permute-start(bf16[32,1,32,256]{3,2,1,0:T(8,128)(2,1)S(1)} %slice.6), channel_id=1, source_target_pairs={{0,8},{8,16},{16,24},{1,9},{9,17},{17,25},{2,10},{10,18},{18,26},{... | collective-permute-start | bytes 1572872 | tf_op jit(solution)/shard_map/ppermute | solution.py:12
  24.7 6.3 %collective-permute-start.1 = (bf16[32,3,1,256]{3,2,1,0:T(2,128)(2,1)S(1)}, bf16[32,3,1,256]{3,2,1,0:T(2,128)(2,1)S(1)}, u32[]{:S(2)}, u32[]{:S(2)}) collective-permute-start(bf16[32,3,1,256]{3,2,1,0:T(2,128)(2,1)S(1)} %slice.12), channel_id=1, source_target_pairs={{0,1},{1,2},{2,3},{3,4},{4,5},{5,6},{6,7},{8,9},{9,10},{10,11},{11... | collective-permute-start | bytes 147464 | tf_op jit(solution)/shard_map/ppermute | solution.py:12
  40.8 12.6 %copy-start.3 = (bf16[3,3,3,32,64]{4,3,2,1,0:T(8,128)(2,1)S(1)}, bf16[3,3,3,32,64]{4,3,2,1,0:T(8,128)(2,1)}, u32[]{:S(2)}) copy-start(bf16[3,3,3,32,64]{4,3,2,1,0:T(8,128)(2,1)} %param.6) | copy-start | bytes 331780
  40.8 12.6 %copy-start.5 = (pred[8,17]{0,1:T(8,128)(4,1)S(1)}, pred[8,17]{0,1:T(8,128)(4,1)}, u32[]{:S(2)}) copy-start(pred[8,17]{0,1:T(8,128)(4,1)} %constant.35) | copy-start | bytes 412
  53.4 6.8 %copy-start.2 = (f32[64]{0:T(128)S(1)}, f32[64]{0:T(128)}, u32[]{:S(2)}) copy-start(f32[64]{0:T(128)} %param.7) | copy-start | bytes 772
  66.9 200.2 %reduce-scatter.4.cloned.1.call-start = ((), (), s32[]{:S(2)}) async-start(), calls=%async_computation.3 | async-start | bytes 5242880
  210.8 4.6 %copy-start.4 = (f32[128]{0:T(128)S(1)}, f32[128]{0:T(128)}, u32[]{:S(2)}) copy-start(f32[128]{0:T(128)} %param.9) | copy-start | bytes 1540
  210.8 59.0 %copy-start.1 = (bf16[3,3,3,64,128]{4,3,2,1,0:T(8,128)(2,1)S(1)}, bf16[3,3,3,64,128]{4,3,2,1,0:T(8,128)(2,1)}, u32[]{:S(2)}) copy-start(bf16[3,3,3,64,128]{4,3,2,1,0:T(8,128)(2,1)} %param.8) | copy-start | bytes 1327108
Sparse Core Ops, SparseCore 0:
  67.0 33.2 all-gather.2
  215.5 51.4 reduce-scatter.3
where the time goes:
time: 280 us; the launch traced here: 277 us
  waiting for transfers between devices  99 us (35%)
  local copies, waits for them, and re-layouts  91.2 us (33%)
  matrix products  55.9 us (20%)
  between operations  13.6 us (5%)
  starting transfers between devices  7.8 us (3%)
  blocking collectives  6.41 us (2%)
    unnamed x3, waiting for transfers between devices  51.6 us
    conv_general_dilated x1, matrix products, on_device(): lax.conv_general_dilated(slab[None], kernel, (1, 1, 1), ((0, 0), (1, 1),...  49.9 us
    conv_general_dilated x3, local copies, waits for them, and re-layouts, on_device(): lax.conv_general_dilated(slab[None], kernel, (1, 1, 1), ((0, 0), (1, 1),...  47.7 us
    all_gather x1, waiting for transfers between devices, on_device(): gathered = lax.all_gather(moved, 'gy', axis=2, tiled=True)  33.3 us
    conv_general_dilated x5, local copies, waits for them, and re-layouts, on_device(): lax.conv_general_dilated(grown[None], conv1_weight, (2, 2, 2), ((0, 0), (...  20.2 us
    ppermute x2, waiting for transfers between devices, shifted(): lax.ppermute(value, axis, [(source, source + steps) for source in range(i...  14.1 us
    broadcast_in_dim x2, local copies, waits for them, and re-layouts, on_device(): slab[None]  7.96 us
    ppermute x2, starting transfers between devices, shifted(): lax.ppermute(value, axis, [(source, source + steps) for source in range(i...  7.76 us
  transfers between devices with their start and end apart: 4, of which 4 were waited for; matrix products, arithmetic and copies ran while one was open for 0% of the time, Pallas kernels for 0%

commit v1 on v0

v1 whole, which is shorter than its diff:
```python
import functools

import jax
import jax.numpy as jnp
from jax import lax
from jax.experimental import pallas as pl
from jax.experimental.pallas import tpu as pltpu
from jax.sharding import PartitionSpec as P

leak_slope = 0.3
MESH = pl.DeviceIdType.MESH
LANES = 128


def leaky(values):
    return jnp.where(values > 0, values, leak_slope * values)


def shift_right(values):
    lane = lax.broadcasted_iota(jnp.int32, values.shape, 1)
    return jnp.where(lane == 0, 0.0, pltpu.roll(values, 1, 1))


def shift_left(values):
    lane = lax.broadcasted_iota(jnp.int32, values.shape, 1)
    return jnp.where(lane == LANES - 1, 0.0, pltpu.roll(values, LANES - 1, 1))


def kernel(groups_x, groups_y, chunks, vol, w1, b1, w2, b2, out,
           cells, part_out, part_in, own, feats, result,
           cell_sems, part_sems, feat_sems, edge_sems, send_sems, recv_sems):
    gx = lax.axis_index("gx")
    gy = lax.axis_index("gy")
    has_left = gx > 0
    has_right = gx < groups_x - 1
    has_up = gy > 0
    has_down = gy < groups_y - 1
    rows = own.shape[0]
    step = rows // chunks
    in_rows = vol.shape[2]
    cin = vol.shape[0]
    cmid = own.shape[1]
    fw = result.shape[2]

    feats[...] = jnp.zeros_like(feats)
    part_in[...] = jnp.zeros_like(part_in)
    cells[0] = jnp.zeros(cells.shape[1:], cells.dtype)

    barrier = pltpu.get_barrier_semaphore()

    def greet(x, y):
        pl.semaphore_signal(barrier, inc=1, device_id=(x, y), device_id_type=MESH)

    for d in range(1, groups_y):
        greet(gx, lax.rem(gy + d, groups_y))
    for dx, okx in ((-1, has_left), (1, has_right)):
        for dy, oky in ((-1, has_up), (0, None), (1, has_down)):
            @pl.when(okx if oky is None else jnp.logical_and(okx, oky))
            def _():
                greet(gx + dx, gy + dy)

    sides_y = 1 + has_up.astype(jnp.int32) + has_down.astype(jnp.int32)
    sides_x = has_left.astype(jnp.int32) + has_right.astype(jnp.int32)

    row = lax.broadcasted_iota(jnp.int32, (2 * LANES, 2 * LANES), 0)
    col = lax.broadcasted_iota(jnp.int32, (2 * LANES, 2 * LANES), 1)
    picked = jnp.where(col < LANES, 2 * col, 2 * col - (2 * LANES - 1))
    select = (row == picked).astype(jnp.float32).astype(jnp.bfloat16)

    def split(block):
        for p in range(2):
            part = vol[:, p, pl.ds(block * 16, 16), :].astype(jnp.float32)
            turned = jnp.swapaxes(part, 0, 1).astype(jnp.bfloat16)
            flat = turned.reshape(16 * cin, 2 * LANES)
            both = jnp.dot(flat, select, preferred_element_type=jnp.float32)
            both = both.astype(jnp.bfloat16)
            for q in range(2):
                cells[pl.ds(1 + block * 16, 16), p, q] = (
                    both[:, q * LANES:(q + 1) * LANES].reshape(16, cin, LANES))

    blocks = in_rows // 16
    split(blocks - 1)
    pl.semaphore_wait(barrier, groups_y - 1 + sides_x * sides_y)

    def cell_copy(y):
        return pltpu.make_async_remote_copy(
            src_ref=cells.at[in_rows], dst_ref=cells.at[0],
            send_sem=cell_sems.at[0], recv_sem=cell_sems.at[1],
            device_id=(gx, y), device_id_type=MESH)

    @pl.when(has_down)
    def _():
        cell_copy(gy + 1).start()

    for block in range(blocks - 1):
        split(block)

    def part_copy(c, x):
        span = pl.ds(c * step, step)
        return pltpu.make_async_remote_copy(
            src_ref=part_out.at[span], dst_ref=part_in.at[span],
            send_sem=part_sems.at[0, c], recv_sem=part_sems.at[1, c],
            device_id=(x, gy), device_id_type=MESH)

    def first_row(j, carry):
        window = cells[pl.ds(2 * j, 3)].reshape(12 * cin, LANES)
        y = jnp.dot(w1[...], window, preferred_element_type=jnp.float32)
        own[j] = y[:cmid] + shift_right(y[cmid:2 * cmid])
        part_out[j] = (y[2 * cmid:3 * cmid] + shift_right(y[3 * cmid:])).astype(jnp.bfloat16)
        return carry

    for c in reversed(range(chunks)):
        if c == 0:
            @pl.when(has_up)
            def _():
                cell_copy(gy).wait_recv()
        lax.fori_loop(c * step, (c + 1) * step, first_row, 0)

        @pl.when(has_right)
        def _():
            part_copy(c, gx + 1).start()

    def feat_copy(c, side, x):
        span = pl.ds(1 + c * step, step)
        return pltpu.make_async_remote_copy(
            src_ref=feats.at[span, 1], dst_ref=feats.at[span, 2 - 2 * side],
            send_sem=feat_sems.at[0, side, c], recv_sem=feat_sems.at[1, side, c],
            device_id=(x, gy), device_id_type=MESH)

    def edge_copy(down, dx, x, y):
        return pltpu.make_async_remote_copy(
            src_ref=feats.at[rows if down else 1, 1],
            dst_ref=feats.at[0 if down else rows + 1, 1 - dx],
            send_sem=edge_sems.at[0, down, dx + 1], recv_sem=edge_sems.at[1, down, dx + 1],
            device_id=(x, y), device_id_type=MESH)

    def both_of(a, b):
        return b if a is None else jnp.logical_and(a, b)

    def send_edges(down):
        for dx, okx in ((0, None), (-1, has_left), (1, has_right)):
            @pl.when(both_of(okx, has_down if down else has_up))
            def _():
                edge_copy(down, dx, gx + dx, gy + (1 if down else -1)).start()

    def finish_row(j, carry):
        value = own[j] + part_in[j].astype(jnp.float32) + b1[...]
        feats[j + 1, 1] = leaky(value).astype(jnp.bfloat16)
        return carry

    for c in reversed(range(chunks)):
        @pl.when(has_left)
        def _():
            part_copy(c, gx).wait_recv()
        lax.fori_loop(c * step, (c + 1) * step, finish_row, 0)
        if c == chunks - 1:
            send_edges(1)
        if c == 0:
            send_edges(0)

        @pl.when(has_left)
        def _():
            feat_copy(c, 0, gx - 1).start()

        @pl.when(has_right)
        def _():
            feat_copy(c, 1, gx + 1).start()

    def result_copy(c, peer, src_group, y, sem_peer):
        span = pl.ds(c * step, step)
        return pltpu.make_async_remote_copy(
            src_ref=result.at[span, peer], dst_ref=out.at[src_group, span],
            send_sem=send_sems.at[c, peer], recv_sem=recv_sems.at[c, sem_peer],
            device_id=(gx, y), device_id_type=MESH)

    def second_row(j, carry):
        window = feats[pl.ds(j, 3)].reshape(9 * cmid, LANES)
        y = jnp.dot(w2[...], window, preferred_element_type=jnp.float32)
        n = y.shape[0] // 3
        total = shift_right(y[:n]) + y[n:2 * n] + shift_left(y[2 * n:]) + b2[...]
        result[j] = leaky(total).reshape(groups_y, fw, LANES).astype(jnp.bfloat16)
        return carry

    def wait_feats(c):
        @pl.when(has_right)
        def _():
            feat_copy(c, 0, gx).wait_recv()

        @pl.when(has_left)
        def _():
            feat_copy(c, 1, gx).wait_recv()

    def wait_edges(down):
        for dx, okx in ((0, None), (-1, has_right), (1, has_left)):
            @pl.when(both_of(okx, has_up if down else has_down))
            def _():
                edge_copy(down, dx, gx, gy).wait_recv()

    wait_feats(chunks - 1)
    wait_edges(0)
    for c in reversed(range(chunks)):
        if c > 0:
            wait_feats(c - 1)
        else:
            wait_edges(1)
        lax.fori_loop(c * step, (c + 1) * step, second_row, 0)

        def send(d, carry):
            peer = lax.rem(gy + d, groups_y)
            result_copy(c, peer, gy, peer, gy).start()
            return carry

        lax.fori_loop(1, groups_y, send, 0)

    out[gy] = result[:, gy]

    @pl.when(has_down)
    def _():
        cell_copy(gy).wait_send()

    for c in range(chunks):
        @pl.when(has_right)
        def _():
            part_copy(c, gx).wait_send()
            feat_copy(c, 1, gx).wait_send()

        @pl.when(has_left)
        def _():
            feat_copy(c, 0, gx).wait_send()

    for down in range(2):
        for dx, okx in ((0, None), (-1, has_left), (1, has_right)):
            @pl.when(both_of(okx, has_down if down else has_up))
            def _():
                edge_copy(down, dx, gx, gy).wait_send()

    for c in reversed(range(chunks)):
        def finish(d, carry):
            peer = lax.rem(gy + d, groups_y)
            copy = result_copy(c, peer, peer, gy, peer)
            copy.wait_send()
            copy.wait_recv()
            return carry

        lax.fori_loop(1, groups_y, finish, 0)


def on_device(volume, conv1_weight, conv1_bias, conv2_weight, conv2_bias):
    groups_x = lax.axis_size("gx")
    groups_y = lax.axis_size("gy")
    cin, planes, in_rows, nz = volume.shape
    cmid = conv1_weight.shape[4]
    cout = conv2_weight.shape[4]
    rows = in_rows // 2
    fw = cout // groups_y
    chunks = 4

    w = conv1_weight.transpose(1, 0, 2, 3, 4)
    own_main = w[:, 1:3, 1:3]
    own_shift = jnp.pad(w[:, 1:3, 0:1], ((0, 0), (0, 0), (1, 0), (0, 0), (0, 0)))
    part_main = jnp.pad(w[:, 0:1, 1:3], ((0, 0), (1, 0), (0, 0), (0, 0), (0, 0)))
    part_shift = jnp.pad(w[:, 0:1, 0:1], ((0, 0), (1, 0), (1, 0), (0, 0), (0, 0)))
    w1 = jnp.concatenate([own_main, own_shift, part_main, part_shift], axis=4)
    w1 = w1.reshape(12 * cin, 4 * cmid).T
    w2 = conv2_weight.transpose(2, 4, 1, 0, 3).reshape(3 * cout, 9 * cmid)

    vmem = pl.BlockSpec(memory_space=pltpu.VMEM)
    moved = pl.pallas_call(
        functools.partial(kernel, groups_x, groups_y, chunks),
        out_shape=jax.ShapeDtypeStruct((groups_y, rows, fw, LANES), jnp.bfloat16),
        in_specs=[vmem] * 5,
        out_specs=vmem,
        scratch_shapes=[
            pltpu.VMEM((in_rows + 1, 2, 2, cin, LANES), jnp.bfloat16),
            pltpu.VMEM((rows, cmid, LANES), jnp.bfloat16),
            pltpu.VMEM((rows, cmid, LANES), jnp.bfloat16),
            pltpu.VMEM((rows, cmid, LANES), jnp.float32),
            pltpu.VMEM((rows + 2, 3, cmid, LANES), jnp.bfloat16),
            pltpu.VMEM((rows, groups_y, fw, LANES), jnp.bfloat16),
            pltpu.SemaphoreType.DMA((2,)),
            pltpu.SemaphoreType.DMA((2, chunks)),
            pltpu.SemaphoreType.DMA((2, 2, chunks)),
            pltpu.SemaphoreType.DMA((2, 2, 3)),
            pltpu.SemaphoreType.DMA((chunks, groups_y)),
            pltpu.SemaphoreType.DMA((chunks, groups_y)),
        ],
        compiler_params=pltpu.CompilerParams(
            collective_id=0, has_side_effects=True, vmem_limit_bytes=40 * 1024 * 1024),
    )(volume, w1, conv1_bias.reshape(cmid, 1), w2, conv2_bias.reshape(cout, 1))
    return moved.transpose(2, 0, 1, 3).reshape(1, fw, groups_y * rows, LANES)


def solution(mesh):
    return jax.shard_map(
        on_device,
        mesh=mesh,
        in_specs=(P(None, "gx", "gy", None), P(), P(), P(), P()),
        out_specs=P("gx", "gy", None, None),
        check_vma=False,
    )
```

time: 280 us -> 41.5 us (0.15)
  waiting for transfers between devices: 99 us -> 0 us
  local copies, waits for them, and re-layouts: 91.2 us -> 4.1 us
  matrix products: 55.9 us -> 0 us
  Pallas kernels: 0 us -> 36.4 us
  between operations: 13.6 us -> 0.11 us
  starting transfers between devices: 7.8 us -> 0 us
  blocking collectives: 6.41 us -> 0 us
    conv_general_dilated x8 -> x0, local copies, waits for them, and re-layouts: 67.9 us -> none  [the longest x3 47.7 us: on_device(): lax.conv_general_dilated(slab[None], kernel, (1, 1, 1), ((0, 0), (1, 1),...]
    conv_general_dilated x2 -> x0, matrix products: 55.9 us -> none  [the longest x1 49.9 us: on_device(): lax.conv_general_dilated(slab[None], kernel, (1, 1, 1), ((0, 0), (1, 1),...]
    unnamed x3 -> x0, waiting for transfers between devices: 51.6 us -> none
    pallas_call x0 -> x1, Pallas kernels: none -> 36.4 us  [on_device(): pl.pallas_call(functools.partial(kernel, groups_x, groups_y, chunks), out...]
    all_gather x1 -> x0, waiting for transfers between devices: 33.3 us -> none  [on_device(): gathered = lax.all_gather(moved, 'gy', axis=2, tiled=True)]
    ppermute x2 -> x0, waiting for transfers between devices: 14.1 us -> none  [shifted(): lax.ppermute(value, axis, [(source, source + steps) for source in range(i...]
    broadcast_in_dim x3 -> x0, local copies, waits for them, and re-layouts: 9.33 us -> none  [the longest x2 7.96 us: on_device(): slab[None]]
    ppermute x2 -> x0, starting transfers between devices: 7.76 us -> none  [shifted(): lax.ppermute(value, axis, [(source, source + steps) for source in range(i...]
  transfers between devices with their start and end apart: 4 -> 0, of which waited for: 4 -> 0; matrix products, arithmetic and copies ran while one was open for 0% -> 0% of each run, Pallas kernels for 0% -> 0%
where the time goes in v1:
time: 41.5 us; the launch traced here: 40.7 us
  Pallas kernels  36.4 us (88%)
  local copies, waits for them, and re-layouts  4.1 us (10%)
    pallas_call x1, Pallas kernels, on_device(): pl.pallas_call(functools.partial(kernel, groups_x, groups_y, chunks), out...  36.4 us
    reshape x2, local copies, waits for them, and re-layouts, on_device(): w2 = conv2_weight.transpose(2, 4, 1, 0, 3).reshape(3 * cout, 9 * cmid)  1.6 us
    unnamed x9, local copies, waits for them, and re-layouts  1.17 us
    reshape x1, local copies, waits for them, and re-layouts, on_device(): return moved.transpose(2, 0, 1, 3).reshape(1, fw, groups_y * rows, LANES)  0.93 us

profile of v1, /device:TPU:5, one launch (start us, length us, event | category | flops | bytes accessed | tf_op | source)
XLA Modules:
  0.0 40.7 jit_solution(10834101723486856219)
XLA Ops:
  0.0 0.0 copy-start.1
  0.0 1.0 %copy.21 = bf16[3,3,3,32,64]{4,3,2,0,1:T(8,128)(2,1)S(1)} copy(bf16[3,3,3,32,64]{4,3,2,1,0:T(8,128)(2,1)} %param.6) | data formatting | bytes 221184 | tf_op args[1]
  1.1 0.1 fusion.6
  1.2 0.2 copy.12
  1.3 0.0 copy-done.1
  1.3 0.8 %copy.18 = bf16[3,128,3,3,64]{4,3,2,1,0:T(4,128)(2,1)S(1)} copy(bf16[3,128,3,3,64]{1,4,0,2,3:T(8,128)(2,1)S(1)} %bitcast.18) | data formatting | bytes 884736 | tf_op jit(solution)/shard_map/reshape | solution.py:265
  2.1 0.0 copy-start.2
  2.1 0.0 copy-start.3
  2.1 0.0 copy-start
  2.1 0.8 %reshape.20.w2 = bf16[384,576]{1,0:T(8,128)(2,1)S(1)} reshape(bf16[3,128,3,3,64]{4,3,2,1,0:T(4,128)(2,1)S(1)} %copy.18) | data formatting | bytes 884736 | tf_op jit(solution)/shard_map/reshape | solution.py:265
  3.0 0.0 copy-done.2
  3.0 0.1 copy.16.b2
  3.1 0.0 copy-done.3
  3.1 0.1 copy.14.b1
  3.2 0.1 copy-done
  3.4 36.4 %shard_map.55 = bf16[8,16,16,128]{3,2,1,0:T(8,128)(2,1)S(1)} custom-call(bf16[32,2,32,256]{3,2,1,0:T(8,128)(2,1)S(1)} %copy-done, bf16[256,384]{1,0:T(8,128)(2,1)S(1)} %bitcast.12, f32[64,1]{1,0:T(8,128)S(1)} %copy.14.b1, bf16[384,576]{1,0:T(8,128)(2,1)S(1)} %reshape.20.w2, f32[128,1]{1,0:T(8,128)S(1)} %copy.16.b2), custom_call_target="tpu_custom_call" | custom-call | tf_op jit(solution)/shard_map/pallas_call | solution.py:268
  39.8 0.9 %copy.17 = bf16[1,16,128,128]{3,2,1,0:T(8,128)(2,1)} copy(bf16[1,16,128,128]{3,1,2,0:T(8,128)(2,1)S(1)} %bitcast.11) | data formatting | bytes 1048576 | tf_op jit(solution)/shard_map/reshape | solution.py:290
  (4 shorter events, 0.0 us)
Async XLA Ops:
  0.0 1.3 %copy-start.1 = (bf16[3,3,3,64,128]{4,3,2,1,0:T(8,128)(2,1)S(1)}, bf16[3,3,3,64,128]{4,3,2,1,0:T(8,128)(2,1)}, u32[]{:S(2)}) copy-start(bf16[3,3,3,64,128]{4,3,2,1,0:T(8,128)(2,1)} %param.8) | copy-start | bytes 1327108
  2.1 0.9 %copy-start.2 = (f32[128]{0:T(128)S(1)}, f32[128]{0:T(128)}, u32[]{:S(2)}) copy-start(f32[128]{0:T(128)} %param.9) | copy-start | bytes 1540
  2.1 1.0 %copy-start.3 = (f32[64]{0:T(128)S(1)}, f32[64]{0:T(128)}, u32[]{:S(2)}) copy-start(f32[64]{0:T(128)} %param.7) | copy-start | bytes 772
  2.1 1.2 %copy-start = (bf16[32,2,32,256]{3,2,1,0:T(8,128)(2,1)S(1)}, bf16[32,2,32,256]{3,2,1,0:T(8,128)(2,1)}, u32[]{:S(2)}) copy-start(bf16[32,2,32,256]{3,2,1,0:T(8,128)(2,1)} %vol.1) | copy-start | bytes 3145732

commit v2 on v1

--- a/solution.py
+++ b/solution.py
@@ -26,8 +26,8 @@
     return jnp.where(lane == LANES - 1, 0.0, pltpu.roll(values, LANES - 1, 1))
 
 
-def kernel(groups_x, groups_y, chunks, vol, w1, b1, w2, b2, out,
-           cells, part_out, part_in, own, feats, result,
+def kernel(groups_x, groups_y, chunks, vol, first_weight, b1, second_weight, b2, out,
+           cells, part_out, part_in, own, own_out, own_in, feats, result, w1, w2,
            cell_sems, part_sems, feat_sems, edge_sems, send_sems, recv_sems):
     gx = lax.axis_index("gx")
     gy = lax.axis_index("gy")
@@ -62,6 +62,20 @@
     sides_y = 1 + has_up.astype(jnp.int32) + has_down.astype(jnp.int32)
     sides_x = has_left.astype(jnp.int32) + has_right.astype(jnp.int32)
 
+    def turned(pieces):
+        return jnp.concatenate(pieces, axis=0).astype(jnp.float32).T.astype(jnp.bfloat16)
+
+    blank = jnp.zeros((cin, cmid), jnp.bfloat16)
+    taps = [(b, p, q) for b in range(3) for p in range(2) for q in range(2)]
+    kinds = (
+        [first_weight[p + 1, b, q + 1] for b, p, q in taps],
+        [first_weight[p + 1, b, 0] if q == 1 else blank for b, p, q in taps],
+        [first_weight[0, b, q + 1] if p == 1 else blank for b, p, q in taps],
+        [first_weight[0, b, 0] if p == 1 and q == 1 else blank for b, p, q in taps],
+    )
+    for place, pieces in enumerate(kinds):
+        w1[place * cmid:(place + 1) * cmid, :] = turned(pieces)
+
     row = lax.broadcasted_iota(jnp.int32, (2 * LANES, 2 * LANES), 0)
     col = lax.broadcasted_iota(jnp.int32, (2 * LANES, 2 * LANES), 1)
     picked = jnp.where(col < LANES, 2 * col, 2 * col - (2 * LANES - 1))
@@ -92,9 +106,6 @@
     def _():
         cell_copy(gy + 1).start()
 
-    for block in range(blocks - 1):
-        split(block)
-
     def part_copy(c, x):
         span = pl.ds(c * step, step)
         return pltpu.make_async_remote_copy(
@@ -102,29 +113,55 @@
             send_sem=part_sems.at[0, c], recv_sem=part_sems.at[1, c],
             device_id=(x, gy), device_id_type=MESH)
 
-    def first_row(j, carry):
-        window = cells[pl.ds(2 * j, 3)].reshape(12 * cin, LANES)
+    def own_copy(c, x):
+        span = pl.ds(c * step, step)
+        return pltpu.make_async_remote_copy(
+            src_ref=own_out.at[span], dst_ref=own_in.at[span],
+            send_sem=feat_sems.at[0, 0, c], recv_sem=feat_sems.at[1, 0, c],
+            device_id=(x, gy), device_id_type=MESH)
+
+    def first_rows(j):
+        window = jnp.concatenate(
+            [cells[2 * (j + h):2 * (j + h) + 3].reshape(12 * cin, LANES) for h in range(2)], axis=1)
         y = jnp.dot(w1[...], window, preferred_element_type=jnp.float32)
-        own[j] = y[:cmid] + shift_right(y[cmid:2 * cmid])
-        part_out[j] = (y[2 * cmid:3 * cmid] + shift_right(y[3 * cmid:])).astype(jnp.bfloat16)
-        return carry
-
+        for h in range(2):
+            z = y[:, h * LANES:(h + 1) * LANES]
+            mine = z[:cmid] + shift_right(z[cmid:2 * cmid])
+            own[j + h] = mine
+            own_out[j + h] = mine.astype(jnp.bfloat16)
+            part_out[j + h] = (
+                z[2 * cmid:3 * cmid] + shift_right(z[3 * cmid:])).astype(jnp.bfloat16)
+
+    ready = blocks - 1
     for c in reversed(range(chunks)):
+        while ready > 0 and 2 * c * step - 1 < ready * 16:
+            ready -= 1
+            split(ready)
         if c == 0:
             @pl.when(has_up)
             def _():
                 cell_copy(gy).wait_recv()
-        lax.fori_loop(c * step, (c + 1) * step, first_row, 0)
+        for j in range(c * step, (c + 1) * step, 2):
+            first_rows(j)
 
         @pl.when(has_right)
         def _():
             part_copy(c, gx + 1).start()
 
-    def feat_copy(c, side, x):
+        @pl.when(has_left)
+        def _():
+            own_copy(c, gx - 1).start()
+
+    filters = w2.shape[0] // 3
+    for e in range(3):
+        w2[e * filters:(e + 1) * filters, :] = turned(
+            [second_weight[a, b, e] for b in range(3) for a in range(3)])
+
+    def feat_copy(c, x):
         span = pl.ds(1 + c * step, step)
         return pltpu.make_async_remote_copy(
-            src_ref=feats.at[span, 1], dst_ref=feats.at[span, 2 - 2 * side],
-            send_sem=feat_sems.at[0, side, c], recv_sem=feat_sems.at[1, side, c],
+            src_ref=feats.at[span, 1], dst_ref=feats.at[span, 0],
+            send_sem=feat_sems.at[0, 1, c], recv_sem=feat_sems.at[1, 1, c],
             device_id=(x, gy), device_id_type=MESH)
 
     def edge_copy(down, dx, x, y):
@@ -158,13 +195,14 @@
         if c == 0:
             send_edges(0)
 
-        @pl.when(has_left)
-        def _():
-            feat_copy(c, 0, gx - 1).start()
-
         @pl.when(has_right)
         def _():
-            feat_copy(c, 1, gx + 1).start()
+            feat_copy(c, gx + 1).start()
+
+    def next_row(j, carry):
+        value = own_in[j].astype(jnp.float32) + part_out[j].astype(jnp.float32) + b1[...]
+        feats[j + 1, 2] = leaky(value).astype(jnp.bfloat16)
+        return carry
 
     def result_copy(c, peer, src_group, y, sem_peer):
         span = pl.ds(c * step, step)
@@ -173,22 +211,25 @@
             send_sem=send_sems.at[c, peer], recv_sem=recv_sems.at[c, sem_peer],
             device_id=(gx, y), device_id_type=MESH)
 
-    def second_row(j, carry):
-        window = feats[pl.ds(j, 3)].reshape(9 * cmid, LANES)
+    def second_rows(j):
+        window = jnp.concatenate(
+            [feats[j + h:j + h + 3].reshape(9 * cmid, LANES) for h in range(2)], axis=1)
         y = jnp.dot(w2[...], window, preferred_element_type=jnp.float32)
-        n = y.shape[0] // 3
-        total = shift_right(y[:n]) + y[n:2 * n] + shift_left(y[2 * n:]) + b2[...]
-        result[j] = leaky(total).reshape(groups_y, fw, LANES).astype(jnp.bfloat16)
-        return carry
+        for h in range(2):
+            z = y[:, h * LANES:(h + 1) * LANES]
+            total = (shift_right(z[:filters]) + z[filters:2 * filters]
+                     + shift_left(z[2 * filters:]) + b2[...])
+            result[j + h] = leaky(total).reshape(groups_y, fw, LANES).astype(jnp.bfloat16)
 
     def wait_feats(c):
         @pl.when(has_right)
         def _():
-            feat_copy(c, 0, gx).wait_recv()
+            own_copy(c, gx).wait_recv()
+            lax.fori_loop(c * step, (c + 1) * step, next_row, 0)
 
         @pl.when(has_left)
         def _():
-            feat_copy(c, 1, gx).wait_recv()
+            feat_copy(c, gx).wait_recv()
 
     def wait_edges(down):
         for dx, okx in ((0, None), (-1, has_right), (1, has_left)):
@@ -203,7 +244,8 @@
             wait_feats(c - 1)
         else:
             wait_edges(1)
-        lax.fori_loop(c * step, (c + 1) * step, second_row, 0)
+        for j in range(c * step, (c + 1) * step, 2):
+            second_rows(j)
 
         def send(d, carry):
             peer = lax.rem(gy + d, groups_y)
@@ -222,11 +264,11 @@
         @pl.when(has_right)
         def _():
             part_copy(c, gx).wait_send()
-            feat_copy(c, 1, gx).wait_send()
+            feat_copy(c, gx).wait_send()
 
         @pl.when(has_left)
         def _():
-            feat_copy(c, 0, gx).wait_send()
+            own_copy(c, gx).wait_send()
 
     for down in range(2):
         for dx, okx in ((0, None), (-1, has_left), (1, has_right)):
@@ -254,15 +296,6 @@
     rows = in_rows // 2
     fw = cout // groups_y
     chunks = 4
-
-    w = conv1_weight.transpose(1, 0, 2, 3, 4)
-    own_main = w[:, 1:3, 1:3]
-    own_shift = jnp.pad(w[:, 1:3, 0:1], ((0, 0), (0, 0), (1, 0), (0, 0), (0, 0)))
-    part_main = jnp.pad(w[:, 0:1, 1:3], ((0, 0), (1, 0), (0, 0), (0, 0), (0, 0)))
-    part_shift = jnp.pad(w[:, 0:1, 0:1], ((0, 0), (1, 0), (1, 0), (0, 0), (0, 0)))
-    w1 = jnp.concatenate([own_main, own_shift, part_main, part_shift], axis=4)
-    w1 = w1.reshape(12 * cin, 4 * cmid).T
-    w2 = conv2_weight.transpose(2, 4, 1, 0, 3).reshape(3 * cout, 9 * cmid)
 
     vmem = pl.BlockSpec(memory_space=pltpu.VMEM)
     moved = pl.pallas_call(
@@ -275,8 +308,12 @@
             pltpu.VMEM((rows, cmid, LANES), jnp.bfloat16),
             pltpu.VMEM((rows, cmid, LANES), jnp.bfloat16),
             pltpu.VMEM((rows, cmid, LANES), jnp.float32),
+            pltpu.VMEM((rows, cmid, LANES), jnp.bfloat16),
+            pltpu.VMEM((rows, cmid, LANES), jnp.bfloat16),
             pltpu.VMEM((rows + 2, 3, cmid, LANES), jnp.bfloat16),
             pltpu.VMEM((rows, groups_y, fw, LANES), jnp.bfloat16),
+            pltpu.VMEM((4 * cmid, 12 * cin), jnp.bfloat16),
+            pltpu.VMEM((3 * cout, 9 * cmid), jnp.bfloat16),
             pltpu.SemaphoreType.DMA((2,)),
             pltpu.SemaphoreType.DMA((2, chunks)),
             pltpu.SemaphoreType.DMA((2, 2, chunks)),
@@ -286,7 +323,7 @@
         ],
         compiler_params=pltpu.CompilerParams(
             collective_id=0, has_side_effects=True, vmem_limit_bytes=40 * 1024 * 1024),
-    )(volume, w1, conv1_bias.reshape(cmid, 1), w2, conv2_bias.reshape(cout, 1))
+    )(volume, conv1_weight, conv1_bias.reshape(cmid, 1), conv2_weight, conv2_bias.reshape(cout, 1))
     return moved.transpose(2, 0, 1, 3).reshape(1, fw, groups_y * rows, LANES)
 
 

time: 41.5 us -> 41.5 us (level); the launches traced: 40.7 us -> 41.3 us
  local copies, waits for them, and re-layouts: 4.1 us -> 5.52 us
  Pallas kernels: 36.4 us -> 35.7 us
    unnamed x9 -> x10, local copies, waits for them, and re-layouts: 1.17 us -> 4.38 us
    reshape x3 -> x0, local copies, waits for them, and re-layouts: 1.77 us -> none  [the longest x2 1.6 us: on_device(): w2 = conv2_weight.transpose(2, 4, 1, 0, 3).reshape(3 * cout, 9 * cmid)]
    pallas_call x1, Pallas kernels: 36.4 us -> 35.7 us  [on_device(): pl.pallas_call(functools.partial(kernel, groups_x, groups_y, chunks), out...]
where the time goes in v2:
time: 41.5 us; the launch traced here: 41.3 us
  Pallas kernels  35.7 us (86%)
  local copies, waits for them, and re-layouts  5.52 us (13%)
    pallas_call x1, Pallas kernels, on_device(): pl.pallas_call(functools.partial(kernel, groups_x, groups_y, chunks), out...  35.7 us
    unnamed x10, local copies, waits for them, and re-layouts  4.38 us
    reshape x1, local copies, waits for them, and re-layouts, on_device(): return moved.transpose(2, 0, 1, 3).reshape(1, fw, groups_y * rows, LANES)  0.93 us

profile of v2, /device:TPU:5, one launch (start us, length us, event | category | flops | bytes accessed | tf_op | source)
XLA Modules:
  0.0 41.3 jit_solution(12780927605226922458)
XLA Ops:
  0.0 0.0 copy-start.3
  0.0 0.7 %copy-done.3 = f32[64]{0:T(128)S(1)} copy-done((f32[64]{0:T(128)S(1)}, f32[64]{0:T(128)}, u32[]{:S(2)}) %copy-start.3) | copy-done | bytes 280
  0.7 0.0 copy-start.4
  0.7 0.1 copy.6.b1
  0.8 0.6 %copy-done.4 = f32[128]{0:T(128)S(1)} copy-done((f32[128]{0:T(128)S(1)}, f32[128]{0:T(128)}, u32[]{:S(2)}) %copy-start.4) | copy-done | bytes 536
  1.3 0.1 copy.7.b2
  1.4 0.0 copy-start
  1.4 1.2 %copy-done = bf16[32,2,32,256]{3,2,1,0:T(8,128)(2,1)S(1)} copy-done((bf16[32,2,32,256]{3,2,1,0:T(8,128)(2,1)S(1)}, bf16[32,2,32,256]{3,2,1,0:T(8,128)(2,1)}, u32[]{:S(2)}) %copy-start) | copy-done | bytes 1048600
  2.6 0.0 copy-start.1
  2.7 1.0 %copy-done.1 = bf16[3,3,3,64,128]{4,3,2,1,0:T(8,128)(2,1)S(1)} copy-done((bf16[3,3,3,64,128]{4,3,2,1,0:T(8,128)(2,1)S(1)}, bf16[3,3,3,64,128]{4,3,2,1,0:T(8,128)(2,1)}, u32[]{:S(2)}) %copy-start.1) | copy-done | bytes 442392
  3.7 0.0 copy-start.2
  3.7 0.9 %copy-done.2 = bf16[3,3,3,32,64]{4,3,2,1,0:T(8,128)(2,1)S(1)} copy-done((bf16[3,3,3,32,64]{4,3,2,1,0:T(8,128)(2,1)S(1)}, bf16[3,3,3,32,64]{4,3,2,1,0:T(8,128)(2,1)}, u32[]{:S(2)}) %copy-start.2) | copy-done | bytes 110616
  4.6 35.7 %shard_map.55 = bf16[8,16,16,128]{3,2,1,0:T(8,128)(2,1)S(1)} custom-call(bf16[32,2,32,256]{3,2,1,0:T(8,128)(2,1)S(1)} %copy-done, bf16[3,3,3,32,64]{4,3,2,1,0:T(8,128)(2,1)S(1)} %copy-done.2, f32[64,1]{1,0:T(8,128)S(1)} %copy.6.b1, bf16[3,3,3,64,128]{4,3,2,1,0:T(8,128)(2,1)S(1)} %copy-done.1, f32[128,1]{1,0:T(8,128)S(1)} %copy.7.b2), custom_call_target="tpu_custom_call" | custom-call | tf_op jit(solution)/shard_map/pallas_call | solution.py:301
  40.3 0.9 %copy.8 = bf16[1,16,128,128]{3,2,1,0:T(8,128)(2,1)} copy(bf16[1,16,128,128]{3,1,2,0:T(8,128)(2,1)S(1)} %bitcast.5) | data formatting | bytes 1048576 | tf_op jit(solution)/shard_map/reshape | solution.py:327
Async XLA Ops:
  0.0 0.7 %copy-start.3 = (f32[64]{0:T(128)S(1)}, f32[64]{0:T(128)}, u32[]{:S(2)}) copy-start(f32[64]{0:T(128)} %param.7) | copy-start | bytes 772
  0.7 0.7 %copy-start.4 = (f32[128]{0:T(128)S(1)}, f32[128]{0:T(128)}, u32[]{:S(2)}) copy-start(f32[128]{0:T(128)} %param.9) | copy-start | bytes 1540
  1.4 1.2 %copy-start = (bf16[32,2,32,256]{3,2,1,0:T(8,128)(2,1)S(1)}, bf16[32,2,32,256]{3,2,1,0:T(8,128)(2,1)}, u32[]{:S(2)}) copy-start(bf16[32,2,32,256]{3,2,1,0:T(8,128)(2,1)} %vol.1) | copy-start | bytes 3145732
  2.6 1.0 %copy-start.1 = (bf16[3,3,3,64,128]{4,3,2,1,0:T(8,128)(2,1)S(1)}, bf16[3,3,3,64,128]{4,3,2,1,0:T(8,128)(2,1)}, u32[]{:S(2)}) copy-start(bf16[3,3,3,64,128]{4,3,2,1,0:T(8,128)(2,1)} %second_weight.1) | copy-start | bytes 1327108
  3.7 0.9 %copy-start.2 = (bf16[3,3,3,32,64]{4,3,2,1,0:T(8,128)(2,1)S(1)}, bf16[3,3,3,32,64]{4,3,2,1,0:T(8,128)(2,1)}, u32[]{:S(2)}) copy-start(bf16[3,3,3,32,64]{4,3,2,1,0:T(8,128)(2,1)} %first_weight.1) | copy-start | bytes 331780

commit v3 on v2

--- a/solution.py
+++ b/solution.py
@@ -26,9 +26,10 @@
     return jnp.where(lane == LANES - 1, 0.0, pltpu.roll(values, LANES - 1, 1))
 
 
-def kernel(groups_x, groups_y, chunks, vol, first_weight, b1, second_weight, b2, out,
-           cells, part_out, part_in, own, own_out, own_in, feats, result, w1, w2,
-           cell_sems, part_sems, feat_sems, edge_sems, send_sems, recv_sems):
+def kernel(groups_x, groups_y, vol_hbm, first_hbm, b1, second_hbm, b2, out,
+           vol, first_weight, second_weight,
+           cells, part_out, part_in, own, feats, result, w1, w2,
+           load_sems, cell_sems, part_sems, feat_sems, edge_sems, send_sems, recv_sems):
     gx = lax.axis_index("gx")
     gy = lax.axis_index("gy")
     has_left = gx > 0
@@ -36,11 +37,24 @@
     has_up = gy > 0
     has_down = gy < groups_y - 1
     rows = own.shape[0]
-    step = rows // chunks
+    step = 2
+    chunks = rows // step
+    order = [chunks - 1, chunks - 2, 0] + list(range(chunks - 3, 0, -1))
+    lag = 2
     in_rows = vol.shape[2]
     cin = vol.shape[0]
     cmid = own.shape[1]
     fw = result.shape[2]
+
+    blocks = in_rows // 16
+    loads = [pltpu.make_async_copy(first_hbm, first_weight, load_sems.at[0])]
+    for block in reversed(range(blocks)):
+        span = pl.ds(block * 16, 16)
+        loads.append(pltpu.make_async_copy(
+            vol_hbm.at[:, :, span], vol.at[:, :, span], load_sems.at[1 + block]))
+    loads.append(pltpu.make_async_copy(second_hbm, second_weight, load_sems.at[1 + blocks]))
+    for load in loads:
+        load.start()
 
     feats[...] = jnp.zeros_like(feats)
     part_in[...] = jnp.zeros_like(part_in)
@@ -61,6 +75,8 @@
 
     sides_y = 1 + has_up.astype(jnp.int32) + has_down.astype(jnp.int32)
     sides_x = has_left.astype(jnp.int32) + has_right.astype(jnp.int32)
+
+    loads[0].wait()
 
     def turned(pieces):
         return jnp.concatenate(pieces, axis=0).astype(jnp.float32).T.astype(jnp.bfloat16)
@@ -82,6 +98,7 @@
     select = (row == picked).astype(jnp.float32).astype(jnp.bfloat16)
 
     def split(block):
+        loads[blocks - block].wait()
         for p in range(2):
             part = vol[:, p, pl.ds(block * 16, 16), :].astype(jnp.float32)
             turned = jnp.swapaxes(part, 0, 1).astype(jnp.bfloat16)
@@ -92,7 +109,6 @@
                 cells[pl.ds(1 + block * 16, 16), p, q] = (
                     both[:, q * LANES:(q + 1) * LANES].reshape(16, cin, LANES))
 
-    blocks = in_rows // 16
     split(blocks - 1)
     pl.semaphore_wait(barrier, groups_y - 1 + sides_x * sides_y)
 
@@ -111,13 +127,6 @@
         return pltpu.make_async_remote_copy(
             src_ref=part_out.at[span], dst_ref=part_in.at[span],
             send_sem=part_sems.at[0, c], recv_sem=part_sems.at[1, c],
-            device_id=(x, gy), device_id_type=MESH)
-
-    def own_copy(c, x):
-        span = pl.ds(c * step, step)
-        return pltpu.make_async_remote_copy(
-            src_ref=own_out.at[span], dst_ref=own_in.at[span],
-            send_sem=feat_sems.at[0, 0, c], recv_sem=feat_sems.at[1, 0, c],
             device_id=(x, gy), device_id_type=MESH)
 
     def first_rows(j):
@@ -126,14 +135,12 @@
         y = jnp.dot(w1[...], window, preferred_element_type=jnp.float32)
         for h in range(2):
             z = y[:, h * LANES:(h + 1) * LANES]
-            mine = z[:cmid] + shift_right(z[cmid:2 * cmid])
-            own[j + h] = mine
-            own_out[j + h] = mine.astype(jnp.bfloat16)
+            own[j + h] = z[:cmid] + shift_right(z[cmid:2 * cmid])
             part_out[j + h] = (
                 z[2 * cmid:3 * cmid] + shift_right(z[3 * cmid:])).astype(jnp.bfloat16)
 
     ready = blocks - 1
-    for c in reversed(range(chunks)):
+    for c in order:
         while ready > 0 and 2 * c * step - 1 < ready * 16:
             ready -= 1
             split(ready)
@@ -141,27 +148,23 @@
             @pl.when(has_up)
             def _():
                 cell_copy(gy).wait_recv()
-        for j in range(c * step, (c + 1) * step, 2):
-            first_rows(j)
+        first_rows(c * step)
 
         @pl.when(has_right)
         def _():
             part_copy(c, gx + 1).start()
 
-        @pl.when(has_left)
-        def _():
-            own_copy(c, gx - 1).start()
-
+    loads[-1].wait()
     filters = w2.shape[0] // 3
     for e in range(3):
         w2[e * filters:(e + 1) * filters, :] = turned(
             [second_weight[a, b, e] for b in range(3) for a in range(3)])
 
-    def feat_copy(c, x):
+    def feat_copy(c, side, x):
         span = pl.ds(1 + c * step, step)
         return pltpu.make_async_remote_copy(
-            src_ref=feats.at[span, 1], dst_ref=feats.at[span, 0],
-            send_sem=feat_sems.at[0, 1, c], recv_sem=feat_sems.at[1, 1, c],
+            src_ref=feats.at[span, 1], dst_ref=feats.at[span, 2 - 2 * side],
+            send_sem=feat_sems.at[0, side, c], recv_sem=feat_sems.at[1, side, c],
             device_id=(x, gy), device_id_type=MESH)
 
     def edge_copy(down, dx, x, y):
@@ -180,32 +183,8 @@
             def _():
                 edge_copy(down, dx, gx + dx, gy + (1 if down else -1)).start()
 
-    def finish_row(j, carry):
-        value = own[j] + part_in[j].astype(jnp.float32) + b1[...]
-        feats[j + 1, 1] = leaky(value).astype(jnp.bfloat16)
-        return carry
-
-    for c in reversed(range(chunks)):
-        @pl.when(has_left)
-        def _():
-            part_copy(c, gx).wait_recv()
-        lax.fori_loop(c * step, (c + 1) * step, finish_row, 0)
-        if c == chunks - 1:
-            send_edges(1)
-        if c == 0:
-            send_edges(0)
-
-        @pl.when(has_right)
-        def _():
-            feat_copy(c, gx + 1).start()
-
-    def next_row(j, carry):
-        value = own_in[j].astype(jnp.float32) + part_out[j].astype(jnp.float32) + b1[...]
-        feats[j + 1, 2] = leaky(value).astype(jnp.bfloat16)
-        return carry
-
     def result_copy(c, peer, src_group, y, sem_peer):
-        span = pl.ds(c * step, step)
+        span = pl.ds(c * 2 * step, 2 * step)
         return pltpu.make_async_remote_copy(
             src_ref=result.at[span, peer], dst_ref=out.at[src_group, span],
             send_sem=send_sems.at[c, peer], recv_sem=recv_sems.at[c, sem_peer],
@@ -221,15 +200,34 @@
                      + shift_left(z[2 * filters:]) + b2[...])
             result[j + h] = leaky(total).reshape(groups_y, fw, LANES).astype(jnp.bfloat16)
 
+    def finish_chunk(c):
+        @pl.when(has_left)
+        def _():
+            part_copy(c, gx).wait_recv()
+        for j in range(c * step, (c + 1) * step):
+            value = own[j] + part_in[j].astype(jnp.float32) + b1[...]
+            feats[j + 1, 1] = leaky(value).astype(jnp.bfloat16)
+
+        @pl.when(has_left)
+        def _():
+            feat_copy(c, 0, gx - 1).start()
+
+        @pl.when(has_right)
+        def _():
+            feat_copy(c, 1, gx + 1).start()
+        if c == chunks - 1:
+            send_edges(1)
+        if c == 0:
+            send_edges(0)
+
     def wait_feats(c):
         @pl.when(has_right)
         def _():
-            own_copy(c, gx).wait_recv()
-            lax.fori_loop(c * step, (c + 1) * step, next_row, 0)
+            feat_copy(c, 0, gx).wait_recv()
 
         @pl.when(has_left)
         def _():
-            feat_copy(c, gx).wait_recv()
+            feat_copy(c, 1, gx).wait_recv()
 
     def wait_edges(down):
         for dx, okx in ((0, None), (-1, has_right), (1, has_left)):
@@ -237,22 +235,38 @@
             def _():
                 edge_copy(down, dx, gx, gy).wait_recv()
 
-    wait_feats(chunks - 1)
-    wait_edges(0)
-    for c in reversed(range(chunks)):
-        if c > 0:
-            wait_feats(c - 1)
-        else:
+    arrived = set()
+
+    def second_chunk(c):
+        for near in (c - 1, c, c + 1):
+            if 0 <= near < chunks and near not in arrived:
+                arrived.add(near)
+                wait_feats(near)
+        if c == chunks - 1:
+            wait_edges(0)
+        if c == 0:
             wait_edges(1)
-        for j in range(c * step, (c + 1) * step, 2):
-            second_rows(j)
-
-        def send(d, carry):
-            peer = lax.rem(gy + d, groups_y)
-            result_copy(c, peer, gy, peer, gy).start()
-            return carry
-
-        lax.fori_loop(1, groups_y, send, 0)
+        second_rows(c * step)
+        if c % 2 == 0:
+            def send(d, carry):
+                peer = lax.rem(gy + d, groups_y)
+                result_copy(c // 2, peer, gy, peer, gy).start()
+                return carry
+
+            lax.fori_loop(1, groups_y, send, 0)
+
+    def ready_at(c):
+        needed = [near for near in (c - 1, c, c + 1) if 0 <= near < chunks]
+        needed.append(0)
+        return max(order.index(near) for near in needed)
+
+    left = list(range(chunks - 1, -1, -1))
+    for place, c in enumerate(order):
+        finish_chunk(c)
+        if left and ready_at(left[0]) + lag <= place:
+            second_chunk(left.pop(0))
+    for c in left:
+        second_chunk(c)
 
     out[gy] = result[:, gy]
 
@@ -264,11 +278,11 @@
         @pl.when(has_right)
         def _():
             part_copy(c, gx).wait_send()
-            feat_copy(c, gx).wait_send()
+            feat_copy(c, 1, gx).wait_send()
 
         @pl.when(has_left)
         def _():
-            own_copy(c, gx).wait_send()
+            feat_copy(c, 0, gx).wait_send()
 
     for down in range(2):
         for dx, okx in ((0, None), (-1, has_left), (1, has_right)):
@@ -276,7 +290,7 @@
             def _():
                 edge_copy(down, dx, gx, gy).wait_send()
 
-    for c in reversed(range(chunks)):
+    for c in reversed(range(chunks // 2)):
         def finish(d, carry):
             peer = lax.rem(gy + d, groups_y)
             copy = result_copy(c, peer, peer, gy, peer)
@@ -295,34 +309,37 @@
     cout = conv2_weight.shape[4]
     rows = in_rows // 2
     fw = cout // groups_y
-    chunks = 4
+    chunks = rows // 2
 
     vmem = pl.BlockSpec(memory_space=pltpu.VMEM)
+    hbm = pl.BlockSpec(memory_space=pltpu.HBM)
     moved = pl.pallas_call(
-        functools.partial(kernel, groups_x, groups_y, chunks),
+        functools.partial(kernel, groups_x, groups_y),
         out_shape=jax.ShapeDtypeStruct((groups_y, rows, fw, LANES), jnp.bfloat16),
-        in_specs=[vmem] * 5,
+        in_specs=[hbm, hbm, vmem, hbm, vmem],
         out_specs=vmem,
         scratch_shapes=[
+            pltpu.VMEM(volume.shape, jnp.bfloat16),
+            pltpu.VMEM(conv1_weight.shape, jnp.bfloat16),
+            pltpu.VMEM(conv2_weight.shape, jnp.bfloat16),
             pltpu.VMEM((in_rows + 1, 2, 2, cin, LANES), jnp.bfloat16),
             pltpu.VMEM((rows, cmid, LANES), jnp.bfloat16),
             pltpu.VMEM((rows, cmid, LANES), jnp.bfloat16),
             pltpu.VMEM((rows, cmid, LANES), jnp.float32),
-            pltpu.VMEM((rows, cmid, LANES), jnp.bfloat16),
-            pltpu.VMEM((rows, cmid, LANES), jnp.bfloat16),
             pltpu.VMEM((rows + 2, 3, cmid, LANES), jnp.bfloat16),
             pltpu.VMEM((rows, groups_y, fw, LANES), jnp.bfloat16),
             pltpu.VMEM((4 * cmid, 12 * cin), jnp.bfloat16),
             pltpu.VMEM((3 * cout, 9 * cmid), jnp.bfloat16),
+            pltpu.SemaphoreType.DMA((2 + in_rows // 16,)),
             pltpu.SemaphoreType.DMA((2,)),
             pltpu.SemaphoreType.DMA((2, chunks)),
             pltpu.SemaphoreType.DMA((2, 2, chunks)),
             pltpu.SemaphoreType.DMA((2, 2, 3)),
-            pltpu.SemaphoreType.DMA((chunks, groups_y)),
-            pltpu.SemaphoreType.DMA((chunks, groups_y)),
+            pltpu.SemaphoreType.DMA((chunks // 2, groups_y)),
+            pltpu.SemaphoreType.DMA((chunks // 2, groups_y)),
         ],
         compiler_params=pltpu.CompilerParams(
-            collective_id=0, has_side_effects=True, vmem_limit_bytes=40 * 1024 * 1024),
+            collective_id=0, has_side_effects=True, vmem_limit_bytes=60 * 1024 * 1024),
     )(volume, conv1_weight, conv1_bias.reshape(cmid, 1), conv2_weight, conv2_bias.reshape(cout, 1))
     return moved.transpose(2, 0, 1, 3).reshape(1, fw, groups_y * rows, LANES)
 

time: 41.5 us -> 40 us (0.964); the launches traced: 41.3 us -> 39.2 us
  local copies, waits for them, and re-layouts: 5.52 us -> 4.07 us
  Pallas kernels: 35.7 us -> 35.1 us
    unnamed x10 -> x4, local copies, waits for them, and re-layouts: 4.38 us -> 0.66 us
    reshape x1, local copies, waits for them, and re-layouts: 0.93 us -> 1.97 us  [on_device(): return moved.transpose(2, 0, 1, 3).reshape(1, fw, groups_y * rows, LANES)]
    pallas_call x1, Pallas kernels: 35.7 us -> 35.1 us  [on_device(): pl.pallas_call(functools.partial(kernel, groups_x, groups_y), out_shape=j...]
    reshape x1, local copies, waits for them, and re-layouts: 0.11 us -> 0.74 us  [on_device(): conv2_bias.reshape(cout, 1)]
    reshape x1, local copies, waits for them, and re-layouts: 0.1 us -> 0.7 us  [on_device(): conv1_bias.reshape(cmid, 1)]
where the time goes in v3:
time: 40 us; the launch traced here: 39.2 us
  Pallas kernels  35.1 us (88%)
  local copies, waits for them, and re-layouts  4.07 us (10%)
    pallas_call x1, Pallas kernels, on_device(): pl.pallas_call(functools.partial(kernel, groups_x, groups_y), out_shape=j...  35.1 us
    reshape x1, local copies, waits for them, and re-layouts, on_device(): return moved.transpose(2, 0, 1, 3).reshape(1, fw, groups_y * rows, LANES)  1.97 us

profile of v3, /device:TPU:5, one launch (start us, length us, event | category | flops | bytes accessed | tf_op | source)
XLA Modules:
  0.0 39.2 jit_solution(14095298333260552170)
XLA Ops:
  0.0 0.0 copy-start
  0.0 0.7 %copy-done = f32[64]{0:T(128)S(1)} copy-done((f32[64]{0:T(128)S(1)}, f32[64]{0:T(128)}, u32[]{:S(2)}) %copy-start) | copy-done | bytes 280
  0.7 0.0 copy-start.1
  0.7 0.7 %copy.6.b1 = f32[64,1]{1,0:T(8,128)} copy(f32[64,1]{0,1:T(1,128)S(1)} %bitcast.6) | data formatting | bytes 512 | tf_op jit(solution)/shard_map/reshape | solution.py:343
  1.4 0.0 copy-done.1
  1.4 0.7 %copy.7.b2 = f32[128,1]{1,0:T(8,128)} copy(f32[128,1]{0,1:T(1,128)S(1)} %bitcast.7) | data formatting | bytes 1024 | tf_op jit(solution)/shard_map/reshape | solution.py:343
  2.1 35.1 %shard_map.55 = bf16[8,16,16,128]{3,2,1,0:T(8,128)(2,1)} custom-call(bf16[32,2,32,256]{3,2,1,0:T(8,128)(2,1)} %vol_hbm.1, bf16[3,3,3,32,64]{4,3,2,1,0:T(8,128)(2,1)} %first_hbm.1, f32[64,1]{1,0:T(8,128)} %copy.6.b1, bf16[3,3,3,64,128]{4,3,2,1,0:T(8,128)(2,1)} %second_hbm.1, f32[128,1]{1,0:T(8,128)} %copy.7.b2), custom_call_target="tpu_custom_call" | custom-call | tf_op jit(solution)/shard_map/pallas_call | solution.py:316
  37.2 2.0 %copy.8 = bf16[1,16,128,128]{3,2,1,0:T(8,128)(2,1)} copy(bf16[1,16,128,128]{3,1,2,0:T(8,128)(2,1)} %bitcast.5) | data formatting | bytes 1048576 | tf_op jit(solution)/shard_map/reshape | solution.py:344
Async XLA Ops:
  0.0 0.7 %copy-start = (f32[64]{0:T(128)S(1)}, f32[64]{0:T(128)}, u32[]{:S(2)}) copy-start(f32[64]{0:T(128)} %param.7) | copy-start | bytes 772
  0.7 0.7 %copy-start.1 = (f32[128]{0:T(128)S(1)}, f32[128]{0:T(128)}, u32[]{:S(2)}) copy-start(f32[128]{0:T(128)} %param.9) | copy-start | bytes 1540

commit v4 on v3

--- a/solution.py
+++ b/solution.py
@@ -26,10 +26,10 @@
     return jnp.where(lane == LANES - 1, 0.0, pltpu.roll(values, LANES - 1, 1))
 
 
-def kernel(groups_x, groups_y, vol_hbm, first_hbm, b1, second_hbm, b2, out,
-           vol, first_weight, second_weight,
+def kernel(groups_x, groups_y, vol_hbm, first_hbm, b1_hbm, second_hbm, b2_hbm, out,
+           vol, first_weight, second_weight, first_bias, second_bias, b1, b2, relay,
            cells, part_out, part_in, own, feats, result, w1, w2,
-           load_sems, cell_sems, part_sems, feat_sems, edge_sems, send_sems, recv_sems):
+           load_sems, cell_sems, part_sems, feat_sems, edge_sems, relay_sems, send_sems, recv_sems):
     gx = lax.axis_index("gx")
     gy = lax.axis_index("gy")
     has_left = gx > 0
@@ -53,6 +53,8 @@
         loads.append(pltpu.make_async_copy(
             vol_hbm.at[:, :, span], vol.at[:, :, span], load_sems.at[1 + block]))
     loads.append(pltpu.make_async_copy(second_hbm, second_weight, load_sems.at[1 + blocks]))
+    loads.append(pltpu.make_async_copy(b1_hbm, first_bias, load_sems.at[2 + blocks]))
+    loads.append(pltpu.make_async_copy(b2_hbm, second_bias, load_sems.at[3 + blocks]))
     for load in loads:
         load.start()
 
@@ -72,6 +74,10 @@
             @pl.when(okx if oky is None else jnp.logical_and(okx, oky))
             def _():
                 greet(gx + dx, gy + dy)
+
+    round_about = groups_x == 4
+    if round_about:
+        greet(lax.rem(gx + 2, 4), gy)
 
     sides_y = 1 + has_up.astype(jnp.int32) + has_down.astype(jnp.int32)
     sides_x = has_left.astype(jnp.int32) + has_right.astype(jnp.int32)
@@ -110,7 +116,7 @@
                     both[:, q * LANES:(q + 1) * LANES].reshape(16, cin, LANES))
 
     split(blocks - 1)
-    pl.semaphore_wait(barrier, groups_y - 1 + sides_x * sides_y)
+    pl.semaphore_wait(barrier, groups_y - 1 + sides_x * sides_y + (1 if round_about else 0))
 
     def cell_copy(y):
         return pltpu.make_async_remote_copy(
@@ -154,7 +160,11 @@
         def _():
             part_copy(c, gx + 1).start()
 
-    loads[-1].wait()
+    for load in loads[-3:]:
+        load.wait()
+    for bias, spread in ((first_bias, b1), (second_bias, b2)):
+        spread[...] = jnp.broadcast_to(bias[...][None, :], (LANES, bias.shape[0])).T
+
     filters = w2.shape[0] // 3
     for e in range(3):
         w2[e * filters:(e + 1) * filters, :] = turned(
@@ -166,6 +176,34 @@
             src_ref=feats.at[span, 1], dst_ref=feats.at[span, 2 - 2 * side],
             send_sem=feat_sems.at[0, side, c], recv_sem=feat_sems.at[1, side, c],
             device_id=(x, gy), device_id_type=MESH)
+
+    def relay_copy(c, x):
+        return pltpu.make_async_remote_copy(
+            src_ref=feats.at[pl.ds(1 + c * step, step), 1], dst_ref=relay.at[pl.ds(c * step, step)],
+            send_sem=relay_sems.at[0, c], recv_sem=relay_sems.at[1, c],
+            device_id=(x, gy), device_id_type=MESH)
+
+    def forward_copy(c, side, x):
+        return pltpu.make_async_remote_copy(
+            src_ref=relay.at[pl.ds(c * step, step)],
+            dst_ref=feats.at[pl.ds(1 + c * step, step), 2 - 2 * side],
+            send_sem=relay_sems.at[2, c], recv_sem=feat_sems.at[1, side, c],
+            device_id=(x, gy), device_id_type=MESH)
+
+    def by_relay(c, side):
+        return round_about and (side == 1 or c % 2 == 1)
+
+    def direct(c, side):
+        there = has_right if side else has_left
+        return jnp.logical_and(there, gx != 2 - side) if by_relay(c, side) else there
+
+    def forward(c):
+        for side, middle in ((1, 3), (0, 0)):
+            if by_relay(c, side):
+                @pl.when(gx == middle)
+                def _():
+                    relay_copy(c, gx).wait_recv()
+                    forward_copy(c, side, 1 + side).start()
 
     def edge_copy(down, dx, x, y):
         return pltpu.make_async_remote_copy(
@@ -208,13 +246,15 @@
             value = own[j] + part_in[j].astype(jnp.float32) + b1[...]
             feats[j + 1, 1] = leaky(value).astype(jnp.bfloat16)
 
-        @pl.when(has_left)
-        def _():
-            feat_copy(c, 0, gx - 1).start()
-
-        @pl.when(has_right)
-        def _():
-            feat_copy(c, 1, gx + 1).start()
+        for side in range(2):
+            @pl.when(direct(c, side))
+            def _():
+                feat_copy(c, side, gx - 1 + 2 * side).start()
+
+            if by_relay(c, side):
+                @pl.when(gx == 2 - side)
+                def _():
+                    relay_copy(c, 3 * side).start()
         if c == chunks - 1:
             send_edges(1)
         if c == 0:
@@ -263,8 +303,11 @@
     left = list(range(chunks - 1, -1, -1))
     for place, c in enumerate(order):
         finish_chunk(c)
+        if place > 0:
+            forward(order[place - 1])
         if left and ready_at(left[0]) + lag <= place:
             second_chunk(left.pop(0))
+    forward(order[-1])
     for c in left:
         second_chunk(c)
 
@@ -278,11 +321,20 @@
         @pl.when(has_right)
         def _():
             part_copy(c, gx).wait_send()
-            feat_copy(c, 1, gx).wait_send()
-
-        @pl.when(has_left)
-        def _():
-            feat_copy(c, 0, gx).wait_send()
+
+        for side in range(2):
+            @pl.when(direct(c, side))
+            def _():
+                feat_copy(c, side, gx).wait_send()
+
+            if by_relay(c, side):
+                @pl.when(gx == 2 - side)
+                def _():
+                    relay_copy(c, gx).wait_send()
+
+                @pl.when(gx == 3 * side)
+                def _():
+                    forward_copy(c, side, gx).wait_send()
 
     for down in range(2):
         for dx, okx in ((0, None), (-1, has_left), (1, has_right)):
@@ -316,12 +368,17 @@
     moved = pl.pallas_call(
         functools.partial(kernel, groups_x, groups_y),
         out_shape=jax.ShapeDtypeStruct((groups_y, rows, fw, LANES), jnp.bfloat16),
-        in_specs=[hbm, hbm, vmem, hbm, vmem],
+        in_specs=[hbm] * 5,
         out_specs=vmem,
         scratch_shapes=[
             pltpu.VMEM(volume.shape, jnp.bfloat16),
             pltpu.VMEM(conv1_weight.shape, jnp.bfloat16),
             pltpu.VMEM(conv2_weight.shape, jnp.bfloat16),
+            pltpu.VMEM((cmid,), jnp.float32),
+            pltpu.VMEM((cout,), jnp.float32),
+            pltpu.VMEM((cmid, LANES), jnp.float32),
+            pltpu.VMEM((cout, LANES), jnp.float32),
+            pltpu.VMEM((rows, cmid, LANES), jnp.bfloat16),
             pltpu.VMEM((in_rows + 1, 2, 2, cin, LANES), jnp.bfloat16),
             pltpu.VMEM((rows, cmid, LANES), jnp.bfloat16),
             pltpu.VMEM((rows, cmid, LANES), jnp.bfloat16),
@@ -330,17 +387,18 @@
             pltpu.VMEM((rows, groups_y, fw, LANES), jnp.bfloat16),
             pltpu.VMEM((4 * cmid, 12 * cin), jnp.bfloat16),
             pltpu.VMEM((3 * cout, 9 * cmid), jnp.bfloat16),
-            pltpu.SemaphoreType.DMA((2 + in_rows // 16,)),
+            pltpu.SemaphoreType.DMA((4 + in_rows // 16,)),
             pltpu.SemaphoreType.DMA((2,)),
             pltpu.SemaphoreType.DMA((2, chunks)),
             pltpu.SemaphoreType.DMA((2, 2, chunks)),
             pltpu.SemaphoreType.DMA((2, 2, 3)),
+            pltpu.SemaphoreType.DMA((3, chunks)),
             pltpu.SemaphoreType.DMA((chunks // 2, groups_y)),
             pltpu.SemaphoreType.DMA((chunks // 2, groups_y)),
         ],
         compiler_params=pltpu.CompilerParams(
             collective_id=0, has_side_effects=True, vmem_limit_bytes=60 * 1024 * 1024),
-    )(volume, conv1_weight, conv1_bias.reshape(cmid, 1), conv2_weight, conv2_bias.reshape(cout, 1))
+    )(volume, conv1_weight, conv1_bias, conv2_weight, conv2_bias)
     return moved.transpose(2, 0, 1, 3).reshape(1, fw, groups_y * rows, LANES)
 
 

time: 40 us -> 37.5 us (0.938)
  the two profiles are of different devices: /device:TPU:5 before, /device:TPU:3 now
where the time goes in v4:
time: 37.5 us; the launch traced here: 37.4 us
  Pallas kernels  35.4 us (94%)
  local copies, waits for them, and re-layouts  1.97 us (5%)
    pallas_call x1, Pallas kernels, on_device(): pl.pallas_call(functools.partial(kernel, groups_x, groups_y), out_shape=j...  35.4 us
    reshape x1, local copies, waits for them, and re-layouts, on_device(): return moved.transpose(2, 0, 1, 3).reshape(1, fw, groups_y * rows, LANES)  1.97 us

profile of v4, /device:TPU:3, one launch (start us, length us, event | category | flops | bytes accessed | tf_op | source)
XLA Modules:
  0.0 37.4 jit_solution(12833718577529052933)
XLA Ops:
  0.0 35.4 %shard_map.55 = bf16[8,16,16,128]{3,2,1,0:T(8,128)(2,1)} custom-call(bf16[32,2,32,256]{3,2,1,0:T(8,128)(2,1)} %vol_hbm.1, bf16[3,3,3,32,64]{4,3,2,1,0:T(8,128)(2,1)} %first_hbm.1, f32[64]{0:T(128)} %b1_hbm.1, bf16[3,3,3,64,128]{4,3,2,1,0:T(8,128)(2,1)} %second_hbm.1, f32[128]{0:T(128)} %b2_hbm.1), custom_call_target="tpu_custom_call" | custom-call | tf_op jit(solution)/shard_map/pallas_call | solution.py:368
  35.4 2.0 %copy.6 = bf16[1,16,128,128]{3,2,1,0:T(8,128)(2,1)} copy(bf16[1,16,128,128]{3,1,2,0:T(8,128)(2,1)} %bitcast.3) | data formatting | bytes 1048576 | tf_op jit(solution)/shard_map/reshape | solution.py:402

commit v5 on v4

--- a/solution.py
+++ b/solution.py
@@ -145,11 +145,13 @@
             part_out[j + h] = (
                 z[2 * cmid:3 * cmid] + shift_right(z[3 * cmid:])).astype(jnp.bfloat16)
 
-    ready = blocks - 1
-    for c in order:
-        while ready > 0 and 2 * c * step - 1 < ready * 16:
-            ready -= 1
-            split(ready)
+    split_blocks = {blocks - 1}
+
+    def first_chunk(c):
+        for block in reversed(range(blocks)):
+            if block not in split_blocks and 2 * c * step - 1 < (block + 1) * 16:
+                split_blocks.add(block)
+                split(block)
         if c == 0:
             @pl.when(has_up)
             def _():
@@ -160,15 +162,19 @@
         def _():
             part_copy(c, gx + 1).start()
 
-    for load in loads[-3:]:
-        load.wait()
-    for bias, spread in ((first_bias, b1), (second_bias, b2)):
-        spread[...] = jnp.broadcast_to(bias[...][None, :], (LANES, bias.shape[0])).T
-
     filters = w2.shape[0] // 3
-    for e in range(3):
-        w2[e * filters:(e + 1) * filters, :] = turned(
-            [second_weight[a, b, e] for b in range(3) for a in range(3)])
+
+    def turn_biases():
+        for load in loads[-2:]:
+            load.wait()
+        for bias, spread in ((first_bias, b1), (second_bias, b2)):
+            spread[...] = jnp.broadcast_to(bias[...][None, :], (LANES, bias.shape[0])).T
+
+    def turn_second_weight():
+        loads[-3].wait()
+        for e in range(3):
+            w2[e * filters:(e + 1) * filters, :] = turned(
+                [second_weight[a, b, e] for b in range(3) for a in range(3)])
 
     def feat_copy(c, side, x):
         span = pl.ds(1 + c * step, step)
@@ -301,13 +307,24 @@
         return max(order.index(near) for near in needed)
 
     left = list(range(chunks - 1, -1, -1))
-    for place, c in enumerate(order):
-        finish_chunk(c)
-        if place > 0:
-            forward(order[place - 1])
-        if left and ready_at(left[0]) + lag <= place:
+    behind = min(3, chunks - 1)
+    turn_biases()
+    for place in range(chunks + behind):
+        if place < chunks:
+            first_chunk(order[place])
+        done = place - behind
+        if done < 0:
+            continue
+        finish_chunk(order[done])
+        if done > 0:
+            forward(order[done - 1])
+        if left and ready_at(left[0]) + lag <= done:
+            if len(left) == chunks:
+                turn_second_weight()
             second_chunk(left.pop(0))
     forward(order[-1])
+    if len(left) == chunks:
+        turn_second_weight()
     for c in left:
         second_chunk(c)
 

time: 37.5 us -> 36.3 us (0.968)
  the two profiles are of different devices: /device:TPU:3 before, /device:TPU:5 now
where the time goes in v5:
time: 36.3 us; the launch traced here: 36.1 us
  Pallas kernels  34.1 us (94%)
  local copies, waits for them, and re-layouts  1.97 us (5%)
    pallas_call x1, Pallas kernels, on_device(): pl.pallas_call(functools.partial(kernel, groups_x, groups_y), out_shape=j...  34.1 us
    reshape x1, local copies, waits for them, and re-layouts, on_device(): return moved.transpose(2, 0, 1, 3).reshape(1, fw, groups_y * rows, LANES)  1.97 us

profile of v5, /device:TPU:5, one launch (start us, length us, event | category | flops | bytes accessed | tf_op | source)
XLA Modules:
  0.0 36.1 jit_solution(12407317279427674551)
XLA Ops:
  0.0 34.1 %shard_map.55 = bf16[8,16,16,128]{3,2,1,0:T(8,128)(2,1)} custom-call(bf16[32,2,32,256]{3,2,1,0:T(8,128)(2,1)} %vol_hbm.1, bf16[3,3,3,32,64]{4,3,2,1,0:T(8,128)(2,1)} %first_hbm.1, f32[64]{0:T(128)} %b1_hbm.1, bf16[3,3,3,64,128]{4,3,2,1,0:T(8,128)(2,1)} %second_hbm.1, f32[128]{0:T(128)} %b2_hbm.1), custom_call_target="tpu_custom_call" | custom-call | tf_op jit(solution)/shard_map/pallas_call | solution.py:385
  34.2 2.0 %copy.6 = bf16[1,16,128,128]{3,2,1,0:T(8,128)(2,1)} copy(bf16[1,16,128,128]{3,1,2,0:T(8,128)(2,1)} %bitcast.3) | data formatting | bytes 1048576 | tf_op jit(solution)/shard_map/reshape | solution.py:419
